TPU v7x, 512 devices: a whole 4x4x16 slice. The times are simulated.
512 devices in a mesh: row: 4 (over z_lo), col: 16 (over z_hi, y), depth: 8 (over x, core).
Axes of the slice: x: 4, y: 4, z: 16 (z_hi: 4, z_lo: 4; z = z_hi * 4 + z_lo), core: 2. Of those that a mesh axis runs over, the one named last changes fastest.
Arguments:
- activations: bfloat16 [8192, 4096], P(('depth', 'row'), 'col'), may hold values from -6 to 6
- gate_grad: bfloat16 [8192, 16384], P(('depth', 'col'), 'row'), may hold values from -6 to 6
- turn_lengths: int32 [64], replicated, may hold values from 1 to 256, 8192 in all
Outputs:
- weight_grad: bfloat16 [4096, 16384], P('col', ('row', 'depth'))
Inputs may be any that keep to these rules, and one draw needn't show every extreme that they name: `turn_lengths`: the 64 lengths sum to 8192; the longest is exactly 256.
All inputs are finite; a program needn't handle non-finite values.
Results may differ from a plain program's by a relative error of at most 0.0043.
Values may be sent and summed in bfloat16 or wider, within the bound.
A program may use at most 64 MiB of HBM per device.

v0:
```python
import jax
import jax.numpy as jnp
from jax import lax
from jax.sharding import PartitionSpec as P


def product_rows(left, right):
    return lax.dot_general(
        left, right, (((0,), (0,)), ((), ())), preferred_element_type=jnp.float32
    )


def local(activations, gate_grad, turn_lengths):
    grad_rows = gate_grad.shape[0]
    group_tokens = grad_rows * lax.axis_size("col")
    first_token = lax.axis_index("depth") * group_tokens + lax.axis_index("col") * grad_rows
    endings = jnp.cumsum(turn_lengths)
    begins = endings - turn_lengths
    token_pos = first_token + jnp.arange(grad_rows, dtype=jnp.int32)
    inside = (token_pos[:, None] >= begins[None, :]) & (token_pos[:, None] < endings[None, :])
    turn_len = jnp.sum(jnp.where(inside, turn_lengths[None, :], 0), axis=1)
    weighted = (gate_grad.astype(jnp.float32) / turn_len.astype(jnp.float32)[:, None]).astype(
        jnp.bfloat16
    )
    gathered = lax.all_gather(activations, "row", axis=0, tiled=True)
    all_grads = lax.all_gather(weighted, "col", axis=0, tiled=True)
    totals = product_rows(gathered, all_grads)
    summed = lax.psum(totals, "depth")
    share = summed.shape[1] // lax.axis_size("depth")
    result = lax.dynamic_slice_in_dim(summed, lax.axis_index("depth") * share, share, 1)
    return result.astype(jnp.bfloat16)


def solution(mesh):
    in_specs = (P(("depth", "row"), "col"), P(("depth", "col"), "row"), P())
    out_specs = P("col", ("row", "depth"))
    return jax.shard_map(local, mesh=mesh, in_specs=in_specs, out_specs=out_specs, check_vma=False)
```

profile of v0, /device:TPU:7, one launch (start us, length us, event | category | flops | bytes accessed | tf_op | source)
XLA Modules:
  0.0 304.3 jit_solution(8354034274886033443)
XLA Ops:
  6.5 0.0 all-gather.2.cloned.1.call-start
  6.5 0.7 copy.8
  7.3 0.1 reduce-window.8
  7.4 0.1 reduce
  7.5 0.7 sub.3
  8.2 0.8 select_reduce_fusion
  9.0 2.1 divide_convert_fusion
  11.1 0.0 all-gather.2.cloned.1.call-update
  11.1 15.7 %all_gather.7 = bf16[1024,256]{1,0:T(8,128)(2,1)S(1)} all-gather(bf16[256,256]{1,0:T(8,128)(2,1)} %param.3), channel_id=1, replica_groups=mesh['row'=4,'col'=16,'depth'=8] {'row'}, dimensions={0}, use_global_device_ids=true | all-gather | bytes 655360 | tf_op jit(solution)/shard_map/all_gather | solution.py:25
  26.8 204.8 %all-gather.2.cloned.1.call-done = bf16[1024,4096]{1,0:T(8,128)(2,1)} async-done(((bf16[64,4096]{1,0:T(8,128)(2,1)}), bf16[1024,4096]{1,0:T(8,128)(2,1)}) %all-gather.2.cloned.1.call-update) | async-done | bytes 8388624 | tf_op jit(solution)/shard_map/all_gather | solution.py:26
  231.6 7.8 %convolution_bitcast_fusion = f32[256,4096]{0,1:T(8,128)} fusion(bf16[1024,4096]{1,0:T(8,128)(2,1)} %all-gather.2.cloned.1.call-done, bf16[1024,256]{1,0:T(8,128)(2,1)S(1)} %all_gather.7), kind=kOutput, calls=%fused_computation | convolution fusion | flops 2147483648 | bytes 13107200 | tf_op jit(solution)/shard_map/dot_general | solution.py:8
  239.4 57.2 %all-reduce.1 = bf16[256,4096]{0,1:T(8,128)(2,1)S(1)} all-reduce(f32[256,4096]{0,1:T(8,128)} %convolution_bitcast_fusion), channel_id=1, replica_groups=mesh['row'=4,'col'=16,'depth'=8] {'depth'}, use_global_device_ids=true, to_apply=%region_2.3 | all-reduce | flops 1048576 | bytes 6291456 | tf_op jit(solution)/shard_map/psum | solution.py:28
  296.6 0.8 copy.9
  (3 shorter events, 0.0 us)
Async XLA Ops:
  6.5 225.0 %all-gather.2.cloned.1.call-start = ((), (), s32[]{:S(2)}) async-start(), calls=%async_computation | async-start | bytes 8912896 | tf_op jit(solution)/shard_map/all_gather | solution.py:26
Sparse Core Ops, SparseCore 0:
  11.2 220.3 all-gather.1
where the time goes:
time: 306 us; the launch traced here: 304 us
  waiting for transfers between devices  205 us (67%)
  blocking collectives  72.9 us (24%)
  between operations  13.4 us (4%)
  matrix products  7.81 us (3%)
  other arithmetic  3.77 us (1%)
    all_gather x1, waiting for transfers between devices, local(): all_grads = lax.all_gather(weighted, 'col', axis=0, tiled=True)  205 us
    psum x1, blocking collectives, local(): summed = lax.psum(totals, 'depth')  57.2 us
    all_gather x1, blocking collectives, local(): gathered = lax.all_gather(activations, 'row', axis=0, tiled=True)  15.7 us
    dot_general x1, matrix products, product_rows(): lax.dot_general(left, right, (((0,), (0,)), ((), ())), preferred_element_...  7.81 us
  transfers between devices with their start and end apart: 1, of which 1 were waited for; matrix products, arithmetic and copies ran while one was open for 0% of the time, Pallas kernels for 0%

commit v1 on v0

v1 whole, which is shorter than its diff:
```python
import jax
import jax.numpy as jnp
from jax import lax
from jax.experimental import pallas as pl
from jax.experimental.pallas import tpu as pltpu
from jax.sharding import PartitionSpec as P

MESH = pl.DeviceIdType.MESH
BF16, F32 = jnp.bfloat16, jnp.float32
HALVES = 2


def kernel(lens_ref, a_ref, g_ref, out_ref, a_mine, w_mine, a_all, w_all, c_out, c_in,
           a_send, a_recv, x_send, x_recv, d_send, d_recv, y_send, y_recv, c_send, c_recv):
    zl = lax.axis_index("row")
    col = lax.axis_index("col")
    depth = lax.axis_index("depth")
    zh, y = lax.div(col, 4), lax.rem(col, 4)
    x, k = lax.div(depth, 2), lax.rem(depth, 2)
    tokens, width = g_ref.shape
    feats = a_ref.shape[1]
    share = width // 8
    half = share // HALVES
    other = 1 - k
    mine = lax.rem(zl + 4 - zh, 4)

    def at(zl_=zl, zh_=zh, y_=y, depth_=depth):
        return (zl_, zh_ * 4 + y_, depth_)

    def turn(value, by):
        return lax.rem(value + by + 4, 4)

    swapped = at(zl_=zh, zh_=zl)
    off_diagonal = zl != zh
    peers = [at(zl_=turn(zl, i)) for i in (1, 2, 3)]
    peers += [at(y_=turn(y, i)) for i in (1, 2, 3)]
    peers += [at(zh_=turn(zh, i)) for i in (1, 3)]
    peers += [at(depth_=lax.rem(depth + i, 8)) for i in range(1, 8)]

    barrier = pltpu.get_barrier_semaphore()
    for peer in peers:
        pl.semaphore_signal(barrier, inc=1, device_id=peer, device_id_type=MESH)

    @pl.when(off_diagonal)
    def _():
        pl.semaphore_signal(barrier, inc=1, device_id=swapped, device_id_type=MESH)

    a_mine[...] = a_ref[...].astype(F32).T.astype(BF16)
    turns = lens_ref.shape[1]
    row = lens_ref[...].astype(F32)
    down = lax.broadcasted_iota(jnp.int32, (turns, turns), 0)
    across = lax.broadcasted_iota(jnp.int32, (turns, turns), 1)
    column = jnp.sum(jnp.where(down == across, row, 0.0), axis=1, keepdims=True)
    endings = jnp.sum(jnp.where(down <= across, column, 0.0), axis=0, keepdims=True)
    begins = endings - row
    token = (lax.broadcasted_iota(jnp.int32, (tokens, turns), 0) + (depth * 16 + col) * tokens).astype(F32)
    inside = (token >= begins) & (token < endings)
    turn_len = jnp.sum(jnp.where(inside, row, 0.0), axis=1, keepdims=True)
    for h in range(HALVES):
        for s in range(8):
            begin = s * share + h * half
            w_mine[h, s] = (g_ref[:, begin:begin + half].astype(F32) / turn_len).astype(BF16)

    pl.semaphore_wait(barrier, jnp.where(off_diagonal, 16, 15))

    sent = []

    def send(src, dst, send_sem, recv_sem, device):
        copy = pltpu.make_async_remote_copy(
            src_ref=src, dst_ref=dst, send_sem=send_sem, recv_sem=recv_sem, device_id=device, device_id_type=MESH)
        copy.start()
        sent.append(copy)

    def arrived(dst, recv_sem):
        pltpu.make_async_remote_copy(
            src_ref=dst, dst_ref=dst, send_sem=a_send.at[0], recv_sem=recv_sem, device_id=peers[0],
            device_id_type=MESH).wait_recv()

    first = pltpu.make_async_remote_copy(
        src_ref=a_mine, dst_ref=a_all.at[lax.rem(zh + 4 - zl, 4), depth], send_sem=a_send.at[0],
        recv_sem=a_recv.at[lax.rem(zh + 4 - zl, 4)], device_id=swapped, device_id_type=MESH)
    stay = pltpu.make_async_copy(a_mine, a_all.at[0, depth], a_recv.at[0])

    @pl.when(off_diagonal)
    def _():
        first.start()

    @pl.when(zl == zh)
    def _():
        stay.start()

    for h in range(HALVES):
        w_keep = pltpu.make_async_copy(w_mine.at[h, depth], w_all.at[h, depth, y], d_recv.at[h, 0])
        w_keep.start()
        for i in (1, 2, 6, 7, 3, 5, 4):
            to = lax.rem(depth + i, 8)
            send(w_mine.at[h, to], w_all.at[h, depth, y], d_send.at[h, i], d_recv.at[h, 8 - i], at(depth_=to))

    def dealt(h):
        pltpu.make_async_copy(w_mine.at[h, depth], w_all.at[h, depth, y], d_recv.at[h, 0]).wait()
        for i in (1, 2, 6, 7, 3, 5, 4):
            s = lax.rem(depth + i, 8)
            arrived(w_all.at[h, s, y], d_recv.at[h, i])

    def gather_y(h):
        for i in (1, 3, 2):
            send(w_all.at[h, :, y], w_all.at[h, :, y], y_send.at[h, i], y_recv.at[h, 4 - i], at(y_=turn(y, i)))

    def gathered_y(h):
        for i in (1, 3, 2):
            part = w_all.at[h, :, turn(y, i)]
            arrived(part, y_recv.at[h, i])

    def spread_x(r):
        piece = a_all.at[r, depth]
        send(piece, piece, x_send.at[r, 0], x_recv.at[r, depth], at(depth_=2 * x + other))
        for n, i in ((1, 1), (2, 3), (3, 2)):
            send(piece, piece, x_send.at[r, n], x_recv.at[r, depth], at(depth_=2 * turn(x, i) + k))

    def forward(r):
        for n, i in ((1, 1), (2, 3), (3, 2)):
            s = 2 * turn(x, i) + k
            piece = a_all.at[r, s]
            arrived(piece, x_recv.at[r, s])
            send(piece, piece, x_send.at[r, 3 + n], x_recv.at[r, s], at(depth_=2 * x + other))

    def complete(r):
        for i in range(4):
            s = 2 * turn(x, i) + other
            arrived(a_all.at[r, s], x_recv.at[r, s])

    def own_first():
        arrived(a_all.at[mine, depth], a_recv.at[mine])
        piece = a_all.at[mine, depth]
        for i in (1, 3, 2):
            send(piece, piece, a_send.at[i], a_recv.at[mine], at(zl_=turn(zl, i)))

    def in_block(r):
        @pl.when(mine != r)
        def _():
            arrived(a_all.at[r, depth], a_recv.at[r])

    def product(r, h):
        total = jnp.dot(a_all[r, 0], w_all[h, 0].reshape(4 * tokens, half), preferred_element_type=F32)
        for s in range(1, 8):
            total += jnp.dot(a_all[r, s], w_all[h, s].reshape(4 * tokens, half), preferred_element_type=F32)
        return total

    up, down_ = at(zh_=turn(zh, 1)), at(zh_=turn(zh, 3))

    def pass_on(n, value, device):
        c_out[n] = value.astype(BF16)
        send(c_out.at[n], c_in.at[n], c_send.at[n], c_recv.at[n], device)

    def came(n):
        arrived(c_in.at[n], c_recv.at[n])
        return c_in[n].astype(F32)

    dealt(0)
    gather_y(0)
    own_first()
    dealt(1)
    gather_y(1)
    in_block(2)
    spread_x(2)
    in_block(3)
    spread_x(3)
    forward(2)
    in_block(1)
    spread_x(1)
    in_block(0)
    spread_x(0)
    complete(2)
    gathered_y(0)
    pass_on(0, product(2, 0), up)
    forward(3)
    complete(3)
    pass_on(3, product(3, 0), down_)
    gathered_y(1)
    pass_on(4, product(2, 1), down_)
    forward(1)
    complete(1)
    pass_on(1, product(1, 1), up)
    pass_on(2, product(1, 0) + came(0), up)
    pass_on(5, product(3, 1) + came(4), down_)
    forward(0)
    complete(0)
    out_ref[:, :half] = (product(0, 0) + came(3) + came(2)).astype(BF16)
    out_ref[:, half:] = (product(0, 1) + came(1) + came(5)).astype(BF16)
    for copy in sent:
        copy.wait_send()

    @pl.when(off_diagonal)
    def _():
        first.wait_send()


def local(activations, gate_grad, turn_lengths):
    tokens, feats = activations.shape
    rows, width = gate_grad.shape
    half = width // 8 // HALVES
    dma = pltpu.SemaphoreType.DMA
    vmem = pl.BlockSpec(memory_space=pltpu.VMEM)
    return pl.pallas_call(
        kernel,
        name="weight_grad",
        out_shape=jax.ShapeDtypeStruct((feats, width // 8), BF16),
        in_specs=[vmem] * 3,
        out_specs=vmem,
        scratch_shapes=[
            pltpu.VMEM((feats, tokens), BF16),
            pltpu.VMEM((HALVES, 8, rows, half), BF16),
            pltpu.VMEM((4, 8, feats, tokens), BF16),
            pltpu.VMEM((HALVES, 8, 4, rows, half), BF16),
            pltpu.VMEM((6, feats, half), BF16),
            pltpu.VMEM((6, feats, half), BF16),
            dma((4,)), dma((4,)),
            dma((4, 7)), dma((4, 8)),
            dma((HALVES, 8)), dma((HALVES, 8)),
            dma((HALVES, 4)), dma((HALVES, 4)),
            dma((6,)), dma((6,)),
        ],
        compiler_params=pltpu.CompilerParams(
            collective_id=0, has_side_effects=True, vmem_limit_bytes=48 * 2**20),
        cost_estimate=pl.CostEstimate(
            flops=2 * 4 * feats * 32 * rows * width // 8, bytes_accessed=2 * (tokens * feats + rows * width),
            transcendentals=0),
    )(turn_lengths.reshape(1, -1), activations, gate_grad)


def solution(mesh):
    in_specs = (P(("depth", "row"), "col"), P(("depth", "col"), "row"), P())
    out_specs = P("col", ("row", "depth"))
    return jax.shard_map(local, mesh=mesh, in_specs=in_specs, out_specs=out_specs, check_vma=False)
```

time: 306 us -> 93.7 us (0.31)
  the two profiles are of different devices: /device:TPU:7 before, /device:TPU:201 now
where the time goes in v1:
time: 93.7 us; the launch traced here: 93.6 us
  Pallas kernels  90.2 us (96%)
  local copies, waits for them, and re-layouts  3.3 us (4%)
    pallas_call x1, Pallas kernels, local(): pl.pallas_call(kernel, name='weight_grad', out_shape=jax.ShapeDtypeStruct...  90.2 us
    unnamed x7, local copies, waits for them, and re-layouts  3.3 us

profile of v1, /device:TPU:201, one launch (start us, length us, event | category | flops | bytes accessed | tf_op | source)
XLA Modules:
  0.0 93.6 jit_solution(10838978962348645527)
XLA Ops:
  0.0 0.0 copy-start.2
  0.0 0.7 copy-done.2
  0.7 0.0 copy-start
  0.7 1.0 %copy-done = bf16[64,4096]{1,0:T(8,128)(2,1)S(1)} copy-done((bf16[64,4096]{1,0:T(8,128)(2,1)S(1)}, bf16[64,4096]{1,0:T(8,128)(2,1)}, u32[]{:S(2)}) %copy-start) | copy-done | bytes 524312
  1.7 0.0 copy-start.1
  1.7 0.9 copy-done.1
  2.6 90.2 %weight_grad.1 = bf16[256,512]{1,0:T(8,128)(2,1)S(1)} custom-call(s32[1,64]{1,0:T(1,128)S(1)} %bitcast.1, bf16[256,256]{1,0:T(8,128)(2,1)S(1)} %copy-done.1, bf16[64,4096]{1,0:T(8,128)(2,1)S(1)} %copy-done), custom_call_target="tpu_custom_call" | custom-call | flops 2147483648 | bytes 655360 | tf_op jit(solution)/shard_map/weight_grad/pallas_call | solution.py:204
  92.9 0.7 copy.5
Async XLA Ops:
  0.0 0.7 copy-start.2
  0.7 1.0 %copy-start = (bf16[64,4096]{1,0:T(8,128)(2,1)S(1)}, bf16[64,4096]{1,0:T(8,128)(2,1)}, u32[]{:S(2)}) copy-start(bf16[64,4096]{1,0:T(8,128)(2,1)} %g_ref.1) | copy-start | bytes 1572868
  1.7 0.9 copy-start.1

commit v2 on v1

v2 whole, which is shorter than its diff:
```python
import jax
import jax.numpy as jnp
from jax import lax
from jax.experimental import pallas as pl
from jax.experimental.pallas import tpu as pltpu
from jax.sharding import PartitionSpec as P

MESH = pl.DeviceIdType.MESH
BF16, F32 = jnp.bfloat16, jnp.float32
HALVES = 2


def kernel(lens_hbm, a_hbm, g_hbm, out_ref, lens_ref, a_ref, g_ref, a_mine, w_mine, a_all, w_all, c_out, c_in,
           in_sem, a_send, a_recv, x_send, x_recv, d_send, d_recv, y_send, y_recv, c_send, c_recv):
    zl = lax.axis_index("row")
    col = lax.axis_index("col")
    depth = lax.axis_index("depth")
    zh, y = lax.div(col, 4), lax.rem(col, 4)
    x, k = lax.div(depth, 2), lax.rem(depth, 2)
    tokens, width = g_ref.shape
    feats = a_ref.shape[1]
    some = feats // HALVES
    share = width // 8
    half = share // HALVES
    other = 1 - k
    mine = lax.rem(zl + 4 - zh, 4)
    theirs = lax.rem(zh + 4 - zl, 4)

    def at(zl_=zl, zh_=zh, y_=y, depth_=depth):
        return (zl_, zh_ * 4 + y_, depth_)

    def turn(value, by):
        return lax.rem(value + by + 4, 4)

    swapped = at(zl_=zh, zh_=zl)
    off_diagonal = zl != zh
    peers = [at(zl_=turn(zl, i)) for i in (1, 2, 3)]
    peers += [at(y_=turn(y, i)) for i in (1, 3)]
    peers += [at(zh_=turn(zh, i)) for i in (1, 3)]
    peers += [at(depth_=lax.rem(depth + i, 8)) for i in range(1, 8)]

    barrier = pltpu.get_barrier_semaphore()
    loads = [pltpu.make_async_copy(src, dst, in_sem.at[n])
             for n, (src, dst) in enumerate(((lens_hbm, lens_ref), (a_hbm, a_ref), (g_hbm, g_ref)))]
    for load in loads:
        load.start()
    for peer in peers:
        pl.semaphore_signal(barrier, inc=1, device_id=peer, device_id_type=MESH)

    @pl.when(off_diagonal)
    def _():
        pl.semaphore_signal(barrier, inc=1, device_id=swapped, device_id_type=MESH)

    loads[0].wait()
    turns = lens_ref.shape[1]
    row = lens_ref[...].astype(F32)
    down = lax.broadcasted_iota(jnp.int32, (turns, turns), 0)
    across = lax.broadcasted_iota(jnp.int32, (turns, turns), 1)
    column = jnp.sum(jnp.where(down == across, row, 0.0), axis=1, keepdims=True)
    endings = jnp.sum(jnp.where(down <= across, column, 0.0), axis=0, keepdims=True)
    begins = endings - row
    token = (lax.broadcasted_iota(jnp.int32, (tokens, turns), 0) + (depth * 16 + col) * tokens).astype(F32)
    inside = (token >= begins) & (token < endings)
    turn_len = jnp.sum(jnp.where(inside, row, 0.0), axis=1, keepdims=True)
    loads[1].wait()
    a_mine[...] = a_ref[...].astype(F32).T.astype(BF16)
    loads[2].wait()
    for h in range(HALVES):
        for s in range(8):
            begin = s * share + h * half
            w_mine[h, s] = (g_ref[:, begin:begin + half].astype(F32) / turn_len).astype(BF16)

    pl.semaphore_wait(barrier, jnp.where(off_diagonal, len(peers) + 1, len(peers)))

    sent = []

    def send(src, dst, send_sem, recv_sem, device):
        copy = pltpu.make_async_remote_copy(
            src_ref=src, dst_ref=dst, send_sem=send_sem, recv_sem=recv_sem, device_id=device, device_id_type=MESH)
        copy.start()
        sent.append(copy)

    def arrived(dst, recv_sem):
        pltpu.make_async_remote_copy(
            src_ref=dst, dst_ref=dst, send_sem=a_send.at[0, 0], recv_sem=recv_sem, device_id=peers[0],
            device_id_type=MESH).wait_recv()

    def part(r, s, e):
        return a_all.at[r, s, pl.ds(e * some, some)]

    first = []
    for e in range(HALVES):
        source = a_mine.at[pl.ds(e * some, some)]
        go = pltpu.make_async_remote_copy(
            src_ref=source, dst_ref=part(theirs, depth, e), send_sem=a_send.at[e, 0],
            recv_sem=a_recv.at[theirs, e], device_id=swapped, device_id_type=MESH)
        stay = pltpu.make_async_copy(source, part(0, depth, e), a_recv.at[0, e])
        first.append(go)
        pl.when(off_diagonal)(go.start)
        pl.when(zl == zh)(stay.start)

    for h in range(HALVES):
        pltpu.make_async_copy(w_mine.at[h, depth], w_all.at[h, depth, y], d_recv.at[h, 0]).start()
        for i in (1, 2, 6, 7, 3, 5, 4):
            to = lax.rem(depth + i, 8)
            send(w_mine.at[h, to], w_all.at[h, depth, y], d_send.at[h, i], d_recv.at[h, 8 - i], at(depth_=to))

    def dealt(h):
        pltpu.make_async_copy(w_mine.at[h, depth], w_all.at[h, depth, y], d_recv.at[h, 0]).wait()
        for i in (1, 2, 6, 7, 3, 5, 4):
            arrived(w_all.at[h, lax.rem(depth + i, 8), y], d_recv.at[h, i])
        whole = w_all.at[h, :, y]
        for n, i in ((0, 1), (1, 3)):
            send(whole, whole, y_send.at[h, n], y_recv.at[h, n], at(y_=turn(y, i)))

    def relay_y(h):
        for n, i, begin in ((0, 1, 0), (1, 3, 4)):
            back = turn(y, 4 - i)
            arrived(w_all.at[h, :, back], y_recv.at[h, n])
            four = w_all.at[h, pl.ds(begin, 4), back]
            send(four, four, y_send.at[h, 2 + n], y_recv.at[h, 2 + n], at(y_=turn(y, i)))

    def gathered_y(h):
        for n, begin in ((0, 0), (1, 4)):
            arrived(w_all.at[h, pl.ds(begin, 4), turn(y, 2)], y_recv.at[h, 2 + n])

    def own_first(e):
        piece = part(mine, depth, e)
        arrived(piece, a_recv.at[mine, e])
        for i in (1, 3, 2):
            send(piece, piece, a_send.at[e, i], a_recv.at[mine, e], at(zl_=turn(zl, i)))

    sibling = at(depth_=2 * x + other)

    def spread_x(r, e):
        piece = part(r, depth, e)

        @pl.when(mine != r)
        def _():
            arrived(piece, a_recv.at[r, e])

        for n, device in ((0, at(depth_=2 * turn(x, 1) + k)), (1, at(depth_=2 * turn(x, 3) + k)), (2, sibling)):
            send(piece, piece, x_send.at[r, e, n], x_recv.at[r, e, depth], device)

    def relay_x(r, e):
        for n, i in ((0, 3), (1, 1)):
            s = 2 * turn(x, i) + k
            piece = part(r, s, e)
            arrived(piece, x_recv.at[r, e, s])
            if n == e:
                send(piece, piece, x_send.at[r, e, 3], x_recv.at[r, e, s], at(depth_=2 * turn(x, 4 - i) + k))
            send(piece, piece, x_send.at[r, e, 4 + n], x_recv.at[r, e, s], sibling)

    def last_x(r, e):
        s = 2 * turn(x, 2) + k
        piece = part(r, s, e)
        arrived(piece, x_recv.at[r, e, s])
        send(piece, piece, x_send.at[r, e, 6], x_recv.at[r, e, s], sibling)

    def complete(r, e):
        for i in (0, 3, 1, 2):
            s = 2 * turn(x, i) + other
            arrived(part(r, s, e), x_recv.at[r, e, s])

    def product(r, e, h):
        total = None
        for s in range(8):
            term = jnp.dot(a_all[r, s, e * some:(e + 1) * some], w_all[h, s].reshape(4 * tokens, half),
                           preferred_element_type=F32)
            total = term if total is None else total + term
        return total

    up, below = at(zh_=turn(zh, 1)), at(zh_=turn(zh, 3))

    def pass_on(n, e, value, device):
        c_out[n, e] = value.astype(BF16)
        send(c_out.at[n, e], c_in.at[n, e], c_send.at[n, e], c_recv.at[n, e], device)

    def came(n, e):
        arrived(c_in.at[n, e], c_recv.at[n, e])
        return c_in[n, e].astype(F32)

    dealt(0)
    own_first(0)
    dealt(1)
    own_first(1)
    spread_x(2, 0)
    spread_x(3, 0)
    relay_y(0)
    relay_x(2, 0)
    relay_x(3, 0)
    spread_x(2, 1)
    spread_x(3, 1)
    last_x(2, 0)
    last_x(3, 0)
    gathered_y(0)
    complete(2, 0)
    pass_on(0, 0, product(2, 0, 0), up)
    complete(3, 0)
    pass_on(3, 0, product(3, 0, 0), below)
    relay_y(1)
    relay_x(2, 1)
    relay_x(3, 1)
    spread_x(1, 0)
    spread_x(1, 1)
    last_x(2, 1)
    last_x(3, 1)
    complete(2, 1)
    pass_on(0, 1, product(2, 1, 0), up)
    complete(3, 1)
    pass_on(3, 1, product(3, 1, 0), below)
    relay_x(1, 0)
    relay_x(1, 1)
    spread_x(0, 0)
    spread_x(0, 1)
    last_x(1, 0)
    last_x(1, 1)
    gathered_y(1)
    pass_on(4, 0, product(2, 0, 1), below)
    complete(1, 0)
    pass_on(1, 0, product(1, 0, 1), up)
    pass_on(4, 1, product(2, 1, 1), below)
    complete(1, 1)
    pass_on(1, 1, product(1, 1, 1), up)
    relay_x(0, 0)
    relay_x(0, 1)
    last_x(0, 0)
    last_x(0, 1)
    for e in range(HALVES):
        pass_on(2, e, product(1, e, 0) + came(0, e), up)
        pass_on(5, e, product(3, e, 1) + came(4, e), below)
    for e in range(HALVES):
        complete(0, e)
    for e in range(HALVES):
        rows = slice(e * some, (e + 1) * some)
        out_ref[rows, :half] = (product(0, e, 0) + came(3, e) + came(2, e)).astype(BF16)
        out_ref[rows, half:] = (product(0, e, 1) + came(1, e) + came(5, e)).astype(BF16)
    for copy in sent:
        copy.wait_send()
    for go in first:
        pl.when(off_diagonal)(go.wait_send)


def local(activations, gate_grad, turn_lengths):
    tokens, feats = activations.shape
    rows, width = gate_grad.shape
    half = width // 8 // HALVES
    dma = pltpu.SemaphoreType.DMA
    return pl.pallas_call(
        kernel,
        name="weight_grad",
        out_shape=jax.ShapeDtypeStruct((feats, width // 8), BF16),
        in_specs=[pl.BlockSpec(memory_space=pl.ANY)] * 3,
        out_specs=pl.BlockSpec(memory_space=pltpu.VMEM),
        scratch_shapes=[
            pltpu.VMEM((1, turn_lengths.shape[0]), jnp.int32),
            pltpu.VMEM((tokens, feats), BF16),
            pltpu.VMEM((rows, width), BF16),
            pltpu.VMEM((feats, tokens), BF16),
            pltpu.VMEM((HALVES, 8, rows, half), BF16),
            pltpu.VMEM((4, 8, feats, tokens), BF16),
            pltpu.VMEM((HALVES, 8, 4, rows, half), BF16),
            pltpu.VMEM((6, HALVES, feats // HALVES, half), BF16),
            pltpu.VMEM((6, HALVES, feats // HALVES, half), BF16),
            dma((3,)),
            dma((HALVES, 4)), dma((4, HALVES)),
            dma((4, HALVES, 7)), dma((4, HALVES, 8)),
            dma((HALVES, 8)), dma((HALVES, 8)),
            dma((HALVES, 4)), dma((HALVES, 4)),
            dma((6, HALVES)), dma((6, HALVES)),
        ],
        compiler_params=pltpu.CompilerParams(
            collective_id=0, has_side_effects=True, vmem_limit_bytes=60 * 2**20),
        cost_estimate=pl.CostEstimate(
            flops=2 * 4 * feats * 32 * rows * width // 8, bytes_accessed=2 * (tokens * feats + rows * width),
            transcendentals=0),
    )(turn_lengths.reshape(1, -1), activations, gate_grad)


def solution(mesh):
    in_specs = (P(("depth", "row"), "col"), P(("depth", "col"), "row"), P())
    out_specs = P("col", ("row", "depth"))
    return jax.shard_map(local, mesh=mesh, in_specs=in_specs, out_specs=out_specs, check_vma=False)
```

time: 93.7 us -> 83.8 us (0.89)
  the two profiles are of different devices: /device:TPU:201 before, /device:TPU:7 now
where the time goes in v2:
time: 83.8 us; the launch traced here: 83.6 us
  Pallas kernels  81.9 us (98%)
  local copies, waits for them, and re-layouts  1.67 us (2%)
    pallas_call x1, Pallas kernels, local(): pl.pallas_call(kernel, name='weight_grad', out_shape=jax.ShapeDtypeStruct...  81.9 us

profile of v2, /device:TPU:7, one launch (start us, length us, event | category | flops | bytes accessed | tf_op | source)
XLA Modules:
  0.0 83.6 jit_solution(4235588254590639117)
XLA Ops:
  0.0 81.9 %weight_grad.1 = bf16[256,512]{1,0:T(8,128)(2,1)} custom-call(s32[1,64]{1,0:T(1,128)} %bitcast.1, bf16[256,256]{1,0:T(8,128)(2,1)} %a_hbm.1, bf16[64,4096]{1,0:T(8,128)(2,1)} %g_hbm.1), custom_call_target="tpu_custom_call" | custom-call | flops 2147483648 | bytes 655360 | tf_op jit(solution)/shard_map/weight_grad/pallas_call | solution.py:249
  82.0 1.7 %copy.5 = bf16[256,512]{1,0:T(8,128)(2,1)} copy(bf16[256,512]{1,0:T(8,128)(2,1)} %weight_grad.1) | data formatting | bytes 524288

commit v3 on v2

v3 whole, which is shorter than its diff:
```python
import jax
import jax.numpy as jnp
from jax import lax
from jax.experimental import pallas as pl
from jax.experimental.pallas import tpu as pltpu
from jax.sharding import PartitionSpec as P

MESH = pl.DeviceIdType.MESH
BF16, F32 = jnp.bfloat16, jnp.float32
FEATS = ((0, 128), (128, 128))
HALVES = 2


def kernel(lens_hbm, a_hbm, g_hbm, out_ref, lens_ref, a_ref, g_ref, a_mine, w_mine, a_all, w_all, c_out, c_in,
           in_sem, a_send, a_recv, x_send, x_recv, d_send, d_recv, y_send, y_recv, c_send, c_recv):
    zl = lax.axis_index("row")
    col = lax.axis_index("col")
    depth = lax.axis_index("depth")
    zh, y = lax.div(col, 4), lax.rem(col, 4)
    x, k = lax.div(depth, 2), lax.rem(depth, 2)
    tokens, width = g_ref.shape
    feats = a_ref.shape[1]
    share = width // 8
    half = share // HALVES
    other = 1 - k

    def slot(piece, block):
        first = jnp.where(piece == 0, 0, lax.rem(piece, 3) + 1)
        fourth = jnp.where(piece == 3, 3, lax.rem(piece + 2, 3))
        return jnp.where(block == 0, first, jnp.where(block == 3, fourth, piece))

    def from_slot(place, block):
        return sum(jnp.where(slot(jnp.int32(piece), block) == place, piece, 0) for piece in range(4))

    source_zh = from_slot(zl, zh)
    mine = lax.rem(source_zh + 4 - zh, 4)
    theirs = lax.rem(zh + 4 - zl, 4)

    def at(zl_=zl, zh_=zh, y_=y, depth_=depth):
        return (zl_, zh_ * 4 + y_, depth_)

    def turn(value, by):
        return lax.rem(value + by + 4, 4)

    target = at(zl_=slot(zh, zl), zh_=zl)
    origin = at(zl_=zh, zh_=source_zh)
    off_diagonal = zl != zh
    comes = source_zh != zh
    peers = [at(zl_=turn(zl, i)) for i in (1, 2, 3)]
    peers += [at(y_=turn(y, i)) for i in (1, 3)]
    peers += [at(zh_=turn(zh, i)) for i in (1, 3)]
    peers += [at(depth_=lax.rem(depth + i, 8)) for i in range(1, 8)]

    barrier = pltpu.get_barrier_semaphore()
    loads = [pltpu.make_async_copy(src, dst, in_sem.at[n])
             for n, (src, dst) in enumerate(((a_hbm, a_ref), (lens_hbm, lens_ref), (g_hbm, g_ref)))]
    for load in loads:
        load.start()
    for peer in peers:
        pl.semaphore_signal(barrier, inc=1, device_id=peer, device_id_type=MESH)

    @pl.when(comes)
    def _():
        pl.semaphore_signal(barrier, inc=1, device_id=origin, device_id_type=MESH)

    loads[0].wait()
    a_mine[...] = a_ref[...].astype(F32).T.astype(BF16)

    pl.semaphore_wait(barrier, jnp.where(off_diagonal, len(peers) + 1, len(peers)))

    sent = []

    def send(src, dst, send_sem, recv_sem, device):
        copy = pltpu.make_async_remote_copy(
            src_ref=src, dst_ref=dst, send_sem=send_sem, recv_sem=recv_sem, device_id=device, device_id_type=MESH)
        copy.start()
        sent.append(copy)

    def arrived(dst, recv_sem):
        pltpu.make_async_remote_copy(
            src_ref=dst, dst_ref=dst, send_sem=a_send.at[0, 0], recv_sem=recv_sem, device_id=peers[0],
            device_id_type=MESH).wait_recv()

    def part(r, s, e):
        return a_all.at[r, s, pl.ds(*FEATS[e])]

    first = []
    for e in range(len(FEATS)):
        source = a_mine.at[pl.ds(*FEATS[e])]
        go = pltpu.make_async_remote_copy(
            src_ref=source, dst_ref=part(theirs, depth, e), send_sem=a_send.at[e, 0],
            recv_sem=a_recv.at[theirs, e], device_id=target, device_id_type=MESH)
        stay = pltpu.make_async_copy(source, part(0, depth, e), a_recv.at[0, e])
        first.append(go)
        pl.when(off_diagonal)(go.start)
        pl.when(zl == zh)(stay.start)

    loads[1].wait()
    turns = lens_ref.shape[1]
    row = lens_ref[...].astype(F32)
    down = lax.broadcasted_iota(jnp.int32, (turns, turns), 0)
    across = lax.broadcasted_iota(jnp.int32, (turns, turns), 1)
    column = jnp.sum(jnp.where(down == across, row, 0.0), axis=1, keepdims=True)
    endings = jnp.sum(jnp.where(down <= across, column, 0.0), axis=0, keepdims=True)
    begins = endings - row
    token = (lax.broadcasted_iota(jnp.int32, (tokens, turns), 0) + (depth * 16 + col) * tokens).astype(F32)
    inside = (token >= begins) & (token < endings)
    turn_len = jnp.sum(jnp.where(inside, row, 0.0), axis=1, keepdims=True)
    loads[2].wait()
    for h in range(HALVES):
        for s in range(8):
            begin = s * share + h * half
            w_mine[h, s] = (g_ref[:, begin:begin + half].astype(F32) / turn_len).astype(BF16)

    for h in range(HALVES):
        pltpu.make_async_copy(w_mine.at[h, depth], w_all.at[h, depth, y], d_recv.at[h, 0]).start()
        for i in (1, 2, 6, 7, 3, 5, 4):
            to = lax.rem(depth + i, 8)
            send(w_mine.at[h, to], w_all.at[h, depth, y], d_send.at[h, i], d_recv.at[h, 8 - i], at(depth_=to))

    def dealt(h):
        pltpu.make_async_copy(w_mine.at[h, depth], w_all.at[h, depth, y], d_recv.at[h, 0]).wait()
        for i in (1, 2, 6, 7, 3, 5, 4):
            arrived(w_all.at[h, lax.rem(depth + i, 8), y], d_recv.at[h, i])
        whole = w_all.at[h, :, y]
        for n, i in ((0, 1), (1, 3)):
            send(whole, whole, y_send.at[h, n], y_recv.at[h, n], at(y_=turn(y, i)))

    def relay_y(h):
        for n, i, begin in ((0, 1, 0), (1, 3, 4)):
            back = turn(y, 4 - i)
            arrived(w_all.at[h, :, back], y_recv.at[h, n])
            four = w_all.at[h, pl.ds(begin, 4), back]
            send(four, four, y_send.at[h, 2 + n], y_recv.at[h, 2 + n], at(y_=turn(y, i)))

    def gathered_y(h):
        for n, begin in ((0, 0), (1, 4)):
            arrived(w_all.at[h, pl.ds(begin, 4), turn(y, 2)], y_recv.at[h, 2 + n])

    def own_first(e):
        piece = part(mine, depth, e)
        arrived(piece, a_recv.at[mine, e])
        for i in (1, 3, 2):
            send(piece, piece, a_send.at[e, i], a_recv.at[mine, e], at(zl_=turn(zl, i)))

    sibling = at(depth_=2 * x + other)

    def spread_x(r, e):
        piece = part(r, depth, e)

        @pl.when(mine != r)
        def _():
            arrived(piece, a_recv.at[r, e])

        for n, i in enumerate((1, 3, 2)):
            send(piece, piece, x_send.at[r, e, n], x_recv.at[r, e, depth], at(depth_=2 * turn(x, i) + k))
        send(piece, piece, x_send.at[r, e, 3], x_recv.at[r, e, depth], sibling)

    def relay_x(r, e):
        for n, i in enumerate((1, 3, 2)):
            s = 2 * turn(x, i) + k
            piece = part(r, s, e)
            arrived(piece, x_recv.at[r, e, s])
            send(piece, piece, x_send.at[r, e, 4 + n], x_recv.at[r, e, s], sibling)

    def complete(r, e):
        for i in (0, 3, 1, 2):
            s = 2 * turn(x, i) + other
            arrived(part(r, s, e), x_recv.at[r, e, s])

    def product(r, e, h):
        total = None
        begin, size = FEATS[e]
        for s in range(8):
            term = jnp.dot(a_all[r, s, begin:begin + size], w_all[h, s].reshape(4 * tokens, half),
                           preferred_element_type=F32)
            total = term if total is None else total + term
        return total

    up, below = at(zh_=turn(zh, 1)), at(zh_=turn(zh, 3))

    def pass_on(n, h, value, device):
        c_out[n, h] = value.astype(BF16)
        send(c_out.at[n, h], c_in.at[n, h], c_send.at[n, h], c_recv.at[n, h], device)

    def came(n, h):
        arrived(c_in.at[n, h], c_recv.at[n, h])
        return c_in[n, h].astype(F32)

    dealt(0)
    own_first(0)
    own_first(1)
    spread_x(2, 0)
    spread_x(3, 0)
    relay_y(0)
    dealt(1)
    relay_x(2, 0)
    relay_x(3, 0)
    spread_x(1, 1)
    spread_x(2, 1)
    spread_x(1, 0)
    spread_x(3, 1)
    gathered_y(0)
    complete(2, 0)
    pass_on(0, 0, product(2, 0, 0), up)
    complete(3, 0)
    pass_on(4, 0, product(3, 0, 0), below)
    relay_x(1, 1)
    relay_x(2, 1)
    relay_y(1)
    complete(2, 1)
    pass_on(3, 0, product(2, 1, 0), below)
    complete(1, 1)
    pass_on(1, 0, product(1, 1, 0), up)
    relay_x(1, 0)
    relay_x(3, 1)
    gathered_y(1)
    pass_on(0, 1, product(2, 0, 1), up)
    pass_on(4, 1, product(3, 0, 1), below)
    pass_on(1, 1, product(1, 1, 1), up)
    pass_on(3, 1, product(2, 1, 1), below)
    spread_x(0, 0)
    spread_x(0, 1)
    complete(1, 0)
    pass_on(2, 0, product(1, 0, 0) + came(0, 0), up)
    pass_on(2, 1, product(1, 0, 1) + came(0, 1), up)
    complete(3, 1)
    pass_on(5, 0, product(3, 1, 0) + came(3, 0), below)
    pass_on(5, 1, product(3, 1, 1) + came(3, 1), below)
    relay_x(0, 0)
    relay_x(0, 1)
    for e in range(len(FEATS)):
        complete(0, e)
    for h in range(HALVES):
        units = pl.ds(h * half, half)
        out_ref[pl.ds(*FEATS[0]), units] = (product(0, 0, h) + came(4, h) + came(2, h)).astype(BF16)
        out_ref[pl.ds(*FEATS[1]), units] = (product(0, 1, h) + came(1, h) + came(5, h)).astype(BF16)
    for copy in sent:
        copy.wait_send()
    for go in first:
        pl.when(off_diagonal)(go.wait_send)


def local(activations, gate_grad, turn_lengths):
    tokens, feats = activations.shape
    rows, width = gate_grad.shape
    share = width // 8
    half = share // 2
    f = len(FEATS)
    dma = pltpu.SemaphoreType.DMA
    return pl.pallas_call(
        kernel,
        name="weight_grad",
        out_shape=jax.ShapeDtypeStruct((feats, width // 8), BF16),
        in_specs=[pl.BlockSpec(memory_space=pl.ANY)] * 3,
        out_specs=pl.BlockSpec(memory_space=pltpu.VMEM),
        scratch_shapes=[
            pltpu.VMEM((1, turn_lengths.shape[0]), jnp.int32),
            pltpu.VMEM((tokens, feats), BF16),
            pltpu.VMEM((rows, width), BF16),
            pltpu.VMEM((feats, tokens), BF16),
            pltpu.VMEM((HALVES, 8, rows, share // HALVES), BF16),
            pltpu.VMEM((4, 8, feats, tokens), BF16),
            pltpu.VMEM((HALVES, 8, 4, rows, share // HALVES), BF16),
            pltpu.VMEM((6, HALVES, feats // 2, half), BF16),
            pltpu.VMEM((6, HALVES, feats // 2, half), BF16),
            dma((3,)),
            dma((f, 4)), dma((4, f)),
            dma((4, f, 7)), dma((4, f, 8)),
            dma((HALVES, 8)), dma((HALVES, 8)),
            dma((HALVES, 4)), dma((HALVES, 4)),
            dma((6, HALVES)), dma((6, HALVES)),
        ],
        compiler_params=pltpu.CompilerParams(
            collective_id=0, has_side_effects=True, vmem_limit_bytes=60 * 2**20),
        cost_estimate=pl.CostEstimate(
            flops=2 * 4 * feats * 32 * rows * width // 8, bytes_accessed=2 * (tokens * feats + rows * width),
            transcendentals=0),
    )(turn_lengths.reshape(1, -1), activations, gate_grad)


def solution(mesh):
    in_specs = (P(("depth", "row"), "col"), P(("depth", "col"), "row"), P())
    out_specs = P("col", ("row", "depth"))
    return jax.shard_map(local, mesh=mesh, in_specs=in_specs, out_specs=out_specs, check_vma=False)
```

time: 83.8 us -> 82 us (0.979)
  the two profiles are of different devices: /device:TPU:7 before, /device:TPU:64 now
where the time goes in v3:
time: 82 us; the launch traced here: 81.8 us
  Pallas kernels  80.2 us (98%)
  local copies, waits for them, and re-layouts  1.67 us (2%)
    pallas_call x1, Pallas kernels, local(): pl.pallas_call(kernel, name='weight_grad', out_shape=jax.ShapeDtypeStruct...  80.2 us
    unnamed x1, local copies, waits for them, and re-layouts  1.67 us

profile of v3, /device:TPU:64, one launch (start us, length us, event | category | flops | bytes accessed | tf_op | source)
XLA Modules:
  0.0 81.8 jit_solution(2657470616688510954)
XLA Ops:
  0.0 80.2 %weight_grad.1 = bf16[256,512]{1,0:T(8,128)(2,1)} custom-call(s32[1,64]{1,0:T(1,128)} %bitcast.1, bf16[256,256]{1,0:T(8,128)(2,1)} %a_hbm.1, bf16[64,4096]{1,0:T(8,128)(2,1)} %g_hbm.1), custom_call_target="tpu_custom_call" | custom-call | flops 2147483648 | bytes 655360 | tf_op jit(solution)/shard_map/weight_grad/pallas_call | solution.py:251
  80.2 1.7 %copy.5 = bf16[256,512]{1,0:T(8,128)(2,1)} copy(bf16[256,512]{1,0:T(8,128)(2,1)} %weight_grad.1) | data formatting | bytes 524288

commit v4 on v3

--- a/solution.py
+++ b/solution.py
@@ -11,7 +11,7 @@
 HALVES = 2
 
 
-def kernel(lens_hbm, a_hbm, g_hbm, out_ref, lens_ref, a_ref, g_ref, a_mine, w_mine, a_all, w_all, c_out, c_in,
+def kernel(lens_hbm, a_hbm, g_hbm, out_ref, lens_ref, a_ref, g_ref, a_mine, w_mine, a_all, w_all, c_out, c_in, total,
            in_sem, a_send, a_recv, x_send, x_recv, d_send, d_recv, y_send, y_recv, c_send, c_recv):
     zl = lax.axis_index("row")
     col = lax.axis_index("col")
@@ -186,6 +186,38 @@
     def came(n, h):
         arrived(c_in.at[n, h], c_recv.at[n, h])
         return c_in[n, h].astype(F32)
+
+    def two_away_last():
+        c_out[3, 1] = product(2, 1, 1).astype(BF16)
+        into = jnp.where(zh == 1, 6, 3)
+        send(c_out.at[3, 1], c_in.at[into, 1], c_send.at[3, 1], c_recv.at[into, 1],
+             at(zh_=turn(zh, jnp.where(zh == 1, 1, 3))))
+
+    def straight_up_last():
+        value = product(1, 1, 1)
+
+        @pl.when(zh == 2)
+        def _():
+            c_out[1, 1] = (value + came(6, 1)).astype(BF16)
+
+        @pl.when(zh != 2)
+        def _():
+            c_out[1, 1] = value.astype(BF16)
+
+        send(c_out.at[1, 1], c_in.at[1, 1], c_send.at[1, 1], c_recv.at[1, 1], up)
+
+    def pass_down_last():
+        value = product(3, 1, 1)
+
+        @pl.when(zh != 0)
+        def _():
+            c_out[5, 1] = (value + came(3, 1)).astype(BF16)
+
+        @pl.when(zh == 0)
+        def _():
+            c_out[5, 1] = value.astype(BF16)
+
+        send(c_out.at[5, 1], c_in.at[5, 1], c_send.at[5, 1], c_recv.at[5, 1], below)
 
     dealt(0)
     own_first(0)
@@ -217,24 +249,27 @@
     gathered_y(1)
     pass_on(0, 1, product(2, 0, 1), up)
     pass_on(4, 1, product(3, 0, 1), below)
-    pass_on(1, 1, product(1, 1, 1), up)
-    pass_on(3, 1, product(2, 1, 1), below)
+    two_away_last()
     spread_x(0, 0)
     spread_x(0, 1)
     complete(1, 0)
     pass_on(2, 0, product(1, 0, 0) + came(0, 0), up)
+    straight_up_last()
     pass_on(2, 1, product(1, 0, 1) + came(0, 1), up)
     complete(3, 1)
     pass_on(5, 0, product(3, 1, 0) + came(3, 0), below)
-    pass_on(5, 1, product(3, 1, 1) + came(3, 1), below)
+    pass_down_last()
     relay_x(0, 0)
     relay_x(0, 1)
     for e in range(len(FEATS)):
         complete(0, e)
+    for e, early in ((0, 4), (1, 1)):
+        for h in range(HALVES):
+            total[pl.ds(*FEATS[e]), pl.ds(h * half, half)] = product(0, e, h) + came(early, h)
     for h in range(HALVES):
-        units = pl.ds(h * half, half)
-        out_ref[pl.ds(*FEATS[0]), units] = (product(0, 0, h) + came(4, h) + came(2, h)).astype(BF16)
-        out_ref[pl.ds(*FEATS[1]), units] = (product(0, 1, h) + came(1, h) + came(5, h)).astype(BF16)
+        for e, late in ((0, 2), (1, 5)):
+            rows, units = pl.ds(*FEATS[e]), pl.ds(h * half, half)
+            out_ref[rows, units] = (total[rows, units] + came(late, h)).astype(BF16)
     for copy in sent:
         copy.wait_send()
     for go in first:
@@ -263,13 +298,14 @@
             pltpu.VMEM((4, 8, feats, tokens), BF16),
             pltpu.VMEM((HALVES, 8, 4, rows, share // HALVES), BF16),
             pltpu.VMEM((6, HALVES, feats // 2, half), BF16),
-            pltpu.VMEM((6, HALVES, feats // 2, half), BF16),
+            pltpu.VMEM((7, HALVES, feats // 2, half), BF16),
+            pltpu.VMEM((feats, share), F32),
             dma((3,)),
             dma((f, 4)), dma((4, f)),
             dma((4, f, 7)), dma((4, f, 8)),
             dma((HALVES, 8)), dma((HALVES, 8)),
             dma((HALVES, 4)), dma((HALVES, 4)),
-            dma((6, HALVES)), dma((6, HALVES)),
+            dma((6, HALVES)), dma((7, HALVES)),
         ],
         compiler_params=pltpu.CompilerParams(
             collective_id=0, has_side_effects=True, vmem_limit_bytes=60 * 2**20),

time: 82 us -> 81.2 us (level)
  the two profiles are of different devices: /device:TPU:64 before, /device:TPU:91 now
where the time goes in v4:
time: 81.2 us; the launch traced here: 81.1 us
  Pallas kernels  79.4 us (98%)
  local copies, waits for them, and re-layouts  1.67 us (2%)
    pallas_call x1, Pallas kernels, local(): pl.pallas_call(kernel, name='weight_grad', out_shape=jax.ShapeDtypeStruct...  79.4 us
    unnamed x1, local copies, waits for them, and re-layouts  1.67 us

profile of v4, /device:TPU:91, one launch (start us, length us, event | category | flops | bytes accessed | tf_op | source)
XLA Modules:
  0.0 81.1 jit_solution(755384095596199336)
XLA Ops:
  0.0 79.4 %weight_grad.1 = bf16[256,512]{1,0:T(8,128)(2,1)} custom-call(s32[1,64]{1,0:T(1,128)} %bitcast.1, bf16[256,256]{1,0:T(8,128)(2,1)} %a_hbm.1, bf16[64,4096]{1,0:T(8,128)(2,1)} %g_hbm.1), custom_call_target="tpu_custom_call" | custom-call | flops 2147483648 | bytes 655360 | tf_op jit(solution)/shard_map/weight_grad/pallas_call | solution.py:286
  79.4 1.7 %copy.5 = bf16[256,512]{1,0:T(8,128)(2,1)} copy(bf16[256,512]{1,0:T(8,128)(2,1)} %weight_grad.1) | data formatting | bytes 524288

commit v5 on v4

--- a/solution.py
+++ b/solution.py
@@ -246,12 +246,12 @@
     pass_on(1, 0, product(1, 1, 0), up)
     relay_x(1, 0)
     relay_x(3, 1)
+    spread_x(0, 0)
+    spread_x(0, 1)
     gathered_y(1)
+    two_away_last()
     pass_on(0, 1, product(2, 0, 1), up)
     pass_on(4, 1, product(3, 0, 1), below)
-    two_away_last()
-    spread_x(0, 0)
-    spread_x(0, 1)
     complete(1, 0)
     pass_on(2, 0, product(1, 0, 0) + came(0, 0), up)
     straight_up_last()

time: 81.2 us -> 80.2 us (0.988)
  the two profiles are of different devices: /device:TPU:91 before, /device:TPU:185 now
where the time goes in v5:
time: 80.2 us; the launch traced here: 80.1 us
  Pallas kernels  78.4 us (98%)
  local copies, waits for them, and re-layouts  1.67 us (2%)
    pallas_call x1, Pallas kernels, local(): pl.pallas_call(kernel, name='weight_grad', out_shape=jax.ShapeDtypeStruct...  78.4 us
    unnamed x1, local copies, waits for them, and re-layouts  1.67 us

profile of v5, /device:TPU:185, one launch (start us, length us, event | category | flops | bytes accessed | tf_op | source)
XLA Modules:
  0.0 80.1 jit_solution(15169171253415865615)
XLA Ops:
  0.0 78.4 %weight_grad.1 = bf16[256,512]{1,0:T(8,128)(2,1)} custom-call(s32[1,64]{1,0:T(1,128)} %bitcast.1, bf16[256,256]{1,0:T(8,128)(2,1)} %a_hbm.1, bf16[64,4096]{1,0:T(8,128)(2,1)} %g_hbm.1), custom_call_target="tpu_custom_call" | custom-call | flops 2147483648 | bytes 655360 | tf_op jit(solution)/shard_map/weight_grad/pallas_call | solution.py:286
  78.4 1.7 %copy.5 = bf16[256,512]{1,0:T(8,128)(2,1)} copy(bf16[256,512]{1,0:T(8,128)(2,1)} %weight_grad.1) | data formatting | bytes 524288
